TPU v7x, 32 devices: a whole 2x2x4 slice. The times are simulated.
32 devices in a mesh: dp: 16 (over z, y, x), mp: 2 (over core).
Axes of the slice: x: 2, y: 2, z: 4, core: 2. Of those that a mesh axis runs over, the one named last changes fastest.
Arguments:
- normed_in: bfloat16 [65536, 512], P(('dp', 'mp')), may hold values from -6 to 6
- dual_in: bfloat16 [65536, 512], P(('dp', 'mp')), may hold values from -6 to 6
- query_weight: bfloat16 [512, 512], P(None, 'mp'), may hold values from -0.25 to 0.25
- key_weight: bfloat16 [512, 512], P(None, 'mp'), may hold values from -0.25 to 0.25
- value_weight: bfloat16 [512, 512], P(None, 'mp'), may hold values from -0.25 to 0.25
- output_weight: bfloat16 [512, 512], P('mp'), may hold values from -3 to 3
- first_gain: float32 [512], replicated, may hold values from 0.25 to 1.75
- first_bias: float32 [512], replicated, may hold values from -3 to 3
- up_weight: bfloat16 [512, 2048], P(None, 'mp'), may hold values from -0.25 to 0.25
- down_weight: bfloat16 [2048, 512], P('mp'), may hold values from -0.125 to 0.125
- second_gain: float32 [512], replicated, may hold values from 0.25 to 1.75
- second_bias: float32 [512], replicated, may hold values from -3 to 3
- segments: int32 [65536], P('dp'), may hold values from 0 to 4, as said below
- grad_normed_out: bfloat16 [65536, 512], P(('dp', 'mp')), may hold values from -12 to 12
- grad_dual_out: bfloat16 [65536, 512], P(('dp', 'mp')), may hold values from -12 to 12
Outputs:
- normed_out: bfloat16 [65536, 512], P(('dp', 'mp'))
- dual_out: bfloat16 [65536, 512], P(('dp', 'mp'))
- grad_normed_in: float32 [65536, 512], P(('dp', 'mp'))
- grad_query: float32 [512, 512], P(None, 'mp')
- grad_key: float32 [512, 512], P(None, 'mp')
- grad_value: float32 [512, 512], P(None, 'mp')
- grad_output: float32 [512, 512], P('mp')
- grad_first_gain: float32 [512], replicated
- grad_first_bias: float32 [512], replicated
- grad_up: float32 [512, 2048], P(None, 'mp')
- grad_down: float32 [2048, 512], P('mp')
- grad_second_gain: float32 [512], replicated
- grad_second_bias: float32 [512], replicated
Inputs may be any that keep to these rules, and one draw needn't show every extreme that they name: `segments`: within each sequence of 1024 tokens the numbers never fall until the padding, which fills the last 1 to 128 positions of every sequence; documents are numbered from 1.
All inputs are finite; a program needn't handle non-finite values.
Results may differ from a plain program's by a relative error of at most 0.013.
The roundings to bfloat16 on the way count: a program that leaves them out, or rounds other values in their place, can miss the bound.
Values may be sent and summed in bfloat16 or wider, within the bound.
No kernel may reach another device: no remote copies, remote signals or barrier semaphores. Data moves between devices by JAX's collectives and lax.ppermute only.
A program may use at most 192 MiB of HBM per device.

v0:
```python
from functools import partial

import jax
import jax.numpy as jnp
from jax import lax
from jax.sharding import PartitionSpec as P

HD = 64
LEN = 1024


norm_eps = 1e-05
masked_score = -1e30


def layer_norm(z, gain, bias):
    mean = jnp.mean(z, axis=-1, keepdims=True)
    centred = z - mean
    spread = jnp.mean(centred * centred, axis=-1, keepdims=True)
    return centred * lax.rsqrt(spread + norm_eps) * gain + bias


def smooth_gate(value):
    return jax.nn.gelu(value, approximate=True)


def split_heads(block, head_size):
    return block.reshape(block.shape[0], block.shape[1] // head_size, head_size).transpose(1, 0, 2)


def join_heads(block):
    return block.transpose(1, 0, 2).reshape(block.shape[1], block.shape[0] * block.shape[2])


def masked_scores(query, keys, labels, head_size):
    raw = jnp.einsum(
        "hqd,hkd->hqk",
        split_heads(query, head_size),
        split_heads(keys, head_size),
        preferred_element_type=jnp.float32,
    ) * head_size ** (-0.5)
    same = labels[:, None] == labels[None, :]
    return jnp.where(same[None], raw, masked_score)


def attend_forward(inputs, head_size):
    query, keys, values, labels = inputs
    scores = masked_scores(query, keys, labels, head_size)
    top = jnp.max(scores, axis=-1, keepdims=True)
    shifted = jnp.exp(scores - top)
    total = jnp.sum(shifted, axis=-1, keepdims=True)
    probs = (shifted / total).astype(jnp.bfloat16)
    mixed = jnp.einsum(
        "hqk,hkd->hqd", probs, split_heads(values, head_size), preferred_element_type=jnp.float32
    )
    live = (labels != 0).astype(jnp.float32)
    return (
        (join_heads(mixed) * live[:, None]).astype(jnp.bfloat16),
        (top + jnp.log(total))[..., 0],
    )


def attend_backward(inputs, head_size):
    query, keys, values, labels, upstream, log_totals = inputs
    scale = head_size ** (-0.5)
    scores = masked_scores(query, keys, labels, head_size)
    probs = jnp.exp(scores - log_totals[..., None])
    live = (labels != 0).astype(jnp.bfloat16)
    grad_mixed = split_heads(upstream * live[:, None], head_size)
    grad_values = jnp.einsum(
        "hqk,hqd->hkd", probs.astype(jnp.bfloat16), grad_mixed, preferred_element_type=jnp.float32
    )
    grad_probs = jnp.einsum(
        "hqd,hkd->hqk",
        grad_mixed,
        split_heads(values, head_size),
        preferred_element_type=jnp.float32,
    )
    grad_scores = (
        probs * (grad_probs - jnp.sum(probs * grad_probs, axis=-1, keepdims=True))
    ).astype(jnp.bfloat16)
    grad_query = (
        jnp.einsum(
            "hqk,hkd->hqd",
            grad_scores,
            split_heads(keys, head_size),
            preferred_element_type=jnp.float32,
        )
        * scale
    )
    grad_keys = (
        jnp.einsum(
            "hqk,hqd->hkd",
            grad_scores,
            split_heads(query, head_size),
            preferred_element_type=jnp.float32,
        )
        * scale
    )
    joined = jnp.concatenate(
        [join_heads(grad_query), join_heads(grad_keys), join_heads(grad_values)], axis=1
    )
    return joined.astype(jnp.bfloat16)


def on_device(
    normed_in,
    dual_in,
    query_weight,
    key_weight,
    value_weight,
    output_weight,
    first_gain,
    first_bias,
    up_weight,
    down_weight,
    second_gain,
    second_bias,
    segments,
    grad_normed_out,
    grad_dual_out,
):
    joint_weight = jnp.concatenate([query_weight, key_weight, value_weight], axis=1)
    att_rows = lax.all_gather(normed_in, "mp", axis=0, tiled=True)
    group = att_rows.shape[0]
    count = group // LEN
    local_width = joint_weight.shape[1] // 3
    qkv = jnp.dot(att_rows, joint_weight, preferred_element_type=jnp.float32).astype(jnp.bfloat16)
    blocks = qkv.reshape(count, LEN, 3 * local_width)
    query = blocks[:, :, :local_width]
    keys = blocks[:, :, local_width : 2 * local_width]
    values = blocks[:, :, 2 * local_width :]
    labels = segments.reshape(count, LEN)
    heads_out, log_totals = lax.map(
        partial(attend_forward, head_size=HD), (query, keys, values, labels)
    )
    heads_out = heads_out.reshape(group, local_width)
    attn = lax.psum_scatter(
        jnp.dot(heads_out, output_weight, preferred_element_type=jnp.float32),
        "mp",
        scatter_dimension=0,
        tiled=True,
    )
    normed, first_pull = jax.vjp(
        layer_norm, normed_in.astype(jnp.float32) + attn, first_gain, first_bias
    )
    dual_mid = dual_in.astype(jnp.float32) + attn
    normed_low = normed.astype(jnp.bfloat16)
    full_up, full_down = (up_weight, down_weight)
    ffn_rows = lax.all_gather(normed_low, "mp", axis=0, tiled=True)
    pre = jnp.dot(ffn_rows, full_up, preferred_element_type=jnp.float32)
    hidden_full, gate_pull = jax.vjp(smooth_gate, pre)
    hidden = hidden_full.astype(jnp.bfloat16)
    ffn_out = lax.psum_scatter(
        jnp.dot(hidden, down_weight, preferred_element_type=jnp.float32),
        "mp",
        scatter_dimension=0,
        tiled=True,
    )
    normed_final, second_pull = jax.vjp(layer_norm, normed + ffn_out, second_gain, second_bias)
    dual_final = dual_mid + ffn_out
    upstream_dual = grad_dual_out.astype(jnp.float32)
    grad_mid, second_gain_part, second_bias_part = second_pull(grad_normed_out.astype(jnp.float32))
    grad_ffn = (grad_mid + upstream_dual).astype(jnp.bfloat16)
    grad_rows = lax.all_gather(grad_ffn, "mp", axis=0, tiled=True)
    grad_hidden = jnp.einsum("td,fd->tf", grad_rows, full_down, preferred_element_type=jnp.float32)
    grad_pre = gate_pull(grad_hidden)[0].astype(jnp.bfloat16)
    down_part = jnp.einsum("tf,td->fd", hidden, grad_rows, preferred_element_type=jnp.float32)
    up_part = jnp.einsum("td,tf->df", ffn_rows, grad_pre, preferred_element_type=jnp.float32)
    piece = grad_pre
    grad_normed = grad_mid + lax.psum_scatter(
        jnp.einsum("tf,df->td", piece, up_weight, preferred_element_type=jnp.float32),
        "mp",
        scatter_dimension=0,
        tiled=True,
    )
    grad_first, first_gain_part, first_bias_part = first_pull(grad_normed)
    grad_attn = (grad_first + upstream_dual).astype(jnp.bfloat16)
    grad_attn_rows = lax.all_gather(grad_attn, "mp", axis=0, tiled=True)
    output_part = jnp.einsum(
        "th,td->hd", heads_out, grad_attn_rows, preferred_element_type=jnp.float32
    )
    grad_heads = jnp.einsum(
        "td,hd->th", grad_attn_rows, output_weight, preferred_element_type=jnp.float32
    ).astype(jnp.bfloat16)
    grad_joint = lax.map(
        partial(attend_backward, head_size=HD),
        (query, keys, values, labels, grad_heads.reshape(count, LEN, local_width), log_totals),
    )
    grad_joint = grad_joint.reshape(group, 3 * local_width)
    joint_part = jnp.einsum("td,tc->dc", att_rows, grad_joint, preferred_element_type=jnp.float32)
    query_part = joint_part[:, :local_width]
    key_part = joint_part[:, local_width : 2 * local_width]
    value_part = joint_part[:, 2 * local_width :]
    piece = grad_joint
    grad_stream = grad_first + lax.psum_scatter(
        jnp.einsum("tc,dc->td", piece, joint_weight, preferred_element_type=jnp.float32).astype(
            jnp.bfloat16
        ),
        "mp",
        scatter_dimension=0,
        tiled=True,
    ).astype(jnp.float32)
    query_total, key_total, value_total, output_total, up_total, down_total = lax.psum(
        (query_part, key_part, value_part, output_part, up_part, down_part), "dp"
    )
    first_gain_total, first_bias_total, second_gain_total, second_bias_total = lax.psum(
        (first_gain_part, first_bias_part, second_gain_part, second_bias_part), ("dp", "mp")
    )
    return (
        normed_final.astype(jnp.bfloat16),
        dual_final.astype(jnp.bfloat16),
        grad_stream,
        query_total,
        key_total,
        value_total,
        output_total,
        first_gain_total,
        first_bias_total,
        up_total,
        down_total,
        second_gain_total,
        second_bias_total,
    )


def solution(mesh):
    return jax.shard_map(
        on_device,
        mesh=mesh,
        in_specs=(
            P(("dp", "mp"), None),
            P(("dp", "mp"), None),
            P(None, "mp"),
            P(None, "mp"),
            P(None, "mp"),
            P("mp", None),
            P(),
            P(),
            P(None, "mp"),
            P("mp", None),
            P(),
            P(),
            P("dp"),
            P(("dp", "mp"), None),
            P(("dp", "mp"), None),
        ),
        out_specs=(
            P(("dp", "mp"), None),
            P(("dp", "mp"), None),
            P(("dp", "mp"), None),
            P(None, "mp"),
            P(None, "mp"),
            P(None, "mp"),
            P("mp", None),
            P(),
            P(),
            P(None, "mp"),
            P("mp", None),
            P(),
            P(),
        ),
        check_vma=False,
    )
```

profile of v0, /device:TPU:0, one launch (start us, length us, event | category | flops | bytes accessed | tf_op | source)
XLA Modules:
  0.0 783.1 jit_solution(6958242161995942423)
XLA Ops:
  11.7 14.3 %all-gather.5.cloned.1.call-done = bf16[4096,512]{1,0:T(8,128)(2,1)} async-done(((bf16[2048,512]{1,0:T(8,128)(2,1)}), bf16[4096,512]{1,0:T(8,128)(2,1)}) %all-gather.5.cloned.1.call-update) | async-done | bytes 4194320 | tf_op jit(solution)/shard_map/all_gather | solution.py:124
  33.7 11.1 %reshape.325 = bf16[4,1024,768]{1,0,2:T(4,128)(2,1)} reshape(bf16[4096,768]{0,1:T(8,128)(2,1)} %fusion.27) | data formatting | bytes 12582912 | tf_op jit(solution)/shard_map/reshape | solution.py:129
  54.9 67.1 %while.22 = (s32[]{:T(128)}, bf16[4,1024,256]{2,1,0:T(8,128)(2,1)}, f32[4,4,1024]{2,1,0:T(4,128)}, s32[4,1024]{1,0:T(4,128)S(1)}, bf16[4,1024,256]{1,2,0:T(8,128...) while((s32[]{:T(128)}, bf16[4,1024,256]{2,1,0:T(8,128)(2,1)}, ...), condition=%wide.region_3.4_spmd, body=%wide.region_0.3_spmd.sunk | while | flops 1125644288 | bytes 64118896 | solution.py:134
  128.4 17.9 %reduce-scatter.5.cloned.1.call-done = f32[2048,512]{1,0:T(8,128)} async-done(((f32[4096,512]{1,0:T(8,128)}), f32[2048,512]{1,0:T(8,128)}) %reduce-scatter.5.cloned.1.call-update) | async-done | bytes 4194320 | tf_op jit(solution)/shard_map/reduce_scatter | solution.py:138
  152.8 15.0 %all-gather.7.cloned.1.call-done = bf16[4096,512]{1,0:T(8,128)(2,1)} async-done(((bf16[2048,512]{1,0:T(8,128)(2,1)}), bf16[4096,512]{1,0:T(8,128)(2,1)}) %all-gather.7.cloned.1.call-update) | async-done | bytes 4194320 | tf_op jit(solution)/shard_map/all_gather | solution.py:150
  167.8 13.5 %multiply_convert_fusion.1 = (bf16[4096,1024]{1,0:T(8,128)(2,1)S(1)}, f32[4096,1024]{1,0:T(8,128)}) fusion(bf16[4096,512]{1,0:T(8,128)(2,1)} %all-gather.7.cloned.1.call-done, bf16[512,1024]{1,0:T(8,128)(2,1)S(1)} %copy-done), kind=kOutput, calls=%fused_computation.54 | convolution fusion | flops 4332716032 | bytes 30408704 | tf_op jit(solution)/shard_map/dot_general | solution.py:151
  191.8 17.7 %reduce-scatter.7.cloned.1.call-done = f32[2048,512]{1,0:T(8,128)} async-done(((f32[4096,512]{1,0:T(8,128)}), f32[2048,512]{1,0:T(8,128)}) %reduce-scatter.7.cloned.1.call-update) | async-done | bytes 4194320 | tf_op jit(solution)/shard_map/reduce_scatter | solution.py:154
  227.0 15.0 %all-gather.9.cloned.1.call-done = bf16[4096,512]{1,0:T(8,128)(2,1)} async-done(((bf16[2048,512]{1,0:T(8,128)(2,1)}), bf16[4096,512]{1,0:T(8,128)(2,1)}) %all-gather.9.cloned.1.call-update) | async-done | bytes 4194320 | tf_op jit(solution)/shard_map/all_gather | solution.py:165
  242.0 17.0 %fusion.26 = bf16[4096,1024]{1,0:T(8,128)(2,1)S(1)} fusion(f32[4096,1024]{1,0:T(8,128)} %get-tuple-element.210, bf16[4096,512]{1,0:T(8,128)(2,1)} %all-gather.9.cloned.1.call-done, bf16[1024,512]{1,0:T(8,128)(2,1)} %param.28), kind=kOutput, calls=%fused_computation.53 | convolution fusion | flops 4378853376 | bytes 30408704 | tf_op jit(solution)/shard_map/td,fd->tf/dot_general | solution.py:166
  269.4 17.9 %reduce-scatter.9.cloned.1.call-done = f32[2048,512]{1,0:T(8,128)} async-done(((f32[4096,512]{1,0:T(8,128)}), f32[2048,512]{1,0:T(8,128)}) %reduce-scatter.9.cloned.1.call-update) | async-done | bytes 4194320 | tf_op jit(solution)/shard_map/reduce_scatter | solution.py:171
  299.3 10.6 %fusion.49 = f32[512,1024]{1,0:T(8,128)} fusion(bf16[4096,512]{1,0:T(8,128)(2,1)} %all-gather.7.cloned.1.call-done, bf16[4096,1024]{1,0:T(8,128)(2,1)} %copy-done.36), kind=kOutput, calls=%fused_computation.108 | convolution fusion | flops 4294967296 | bytes 14680064 | tf_op jit(solution)/shard_map/td,tf->df/dot_general | solution.py:169
  309.9 9.0 %fusion.50 = f32[1024,512]{1,0:T(8,128)} fusion(bf16[4096,1024]{1,0:T(8,128)(2,1)} %copy-done.35, bf16[4096,512]{1,0:T(8,128)(2,1)S(1)} %copy-done.33), kind=kOutput, calls=%fused_computation.109 | convolution fusion | flops 4294967296 | bytes 14680064 | tf_op jit(solution)/shard_map/tf,td->fd/dot_general | solution.py:168
  323.7 202.4 %while.23 = (s32[]{:T(128)}, bf16[4,1024,768]{2,1,0:T(8,128)(2,1)}, s32[4,1024]{1,0:T(4,128)S(1)}, bf16[4,1024,256]{1,2,0:T(8,128)(2,1)}, bf16[4,1024,256]{1,2,0...) while((s32[]{:T(128)}, bf16[4,1024,768]{2,1,0:T(8,128)(2,1)}, ...), condition=%wide.region_17.18_spmd, body=%wide.region_15.17_spmd.sunk | while | flops 2729703424 | bytes 217356560 | solution.py:186
  333.7 11.9 %multiply_reduce_fusion.6 = (f32[4,1024]{1,0:T(4,128)}, f32[4,1024,1024]{1,2,0:T(8,128)}) fusion(f32[4,1024,1024]{1,2,0:T(8,128)S(1)} %fusion.123, f32[4,1024]{1,0:T(4,128)} %dynamic-slice_bitcast_fusion.2, bf16[4,1024,64]{1,2,0:T(8,128)(2,1)} %bitcast.147, bf16[4,1024,64]{1,2,0:T(8,128)(2,1)S(1)} %bitcast.145, ...), kind=kOutput, calls=%fused_computation.19.clone.1 | convolution fusion | flops 557838336 | bytes 35684352 | tf_op jit(solution)/shard_map/while/body/eval_jaxpr/hqd,hkd->hqk/dot_general | solution.py:36
  345.7 8.4 %fusion.124 = bf16[4,1024,64]{1,2,0:T(8,128)(2,1)S(1)} fusion(f32[4,1024,1024]{1,2,0:T(8,128)} %get-tuple-element.317, bf16[1024,4,64]{0,2,1:T(8,128)(2,1)S(1)} %bitcast.144, bf16[1024]{0:T(1024)(128)(2,1)S(1)} %compare_convert_fusion.5), kind=kOutput, calls=%fused_computation.27.clone.1 | convolution fusion | flops 541589504 | bytes 17827840 | tf_op jit(solution)/shard_map/while/body/eval_jaxpr/hqk,hqd->hkd/dot_general | solution.py:70
  354.1 11.7 %multiply_convert_fusion.3 = bf16[4,1024,1024]{1,2,0:T(8,128)(2,1)S(1)} fusion(f32[4,1024,1024]{1,2,0:T(8,128)} %get-tuple-element.317, f32[4,1024,1024]{1,2,0:T(8,128)} %copy-done.2, f32[4,1024]{1,0:T(4,128)S(1)} %copy-done.15), kind=kLoop, calls=%fused_computation.18.clone.1 | loop fusion | flops 12582912 | bytes 41959424 | tf_op jit(solution)/shard_map/while/body/eval_jaxpr/convert_element_type | solution.py:81
  384.3 11.9 %multiply_reduce_fusion.6 = (f32[4,1024]{1,0:T(4,128)}, f32[4,1024,1024]{1,2,0:T(8,128)}) fusion(f32[4,1024,1024]{1,2,0:T(8,128)S(1)} %fusion.123, f32[4,1024]{1,0:T(4,128)} %dynamic-slice_bitcast_fusion.2, bf16[4,1024,64]{1,2,0:T(8,128)(2,1)} %bitcast.147, bf16[4,1024,64]{1,2,0:T(8,128)(2,1)S(1)} %bitcast.145, ...), kind=kOutput, calls=%fused_computation.19.clone.1 | convolution fusion | flops 557838336 | bytes 35684352 | tf_op jit(solution)/shard_map/while/body/eval_jaxpr/hqd,hkd->hqk/dot_general | solution.py:36
  404.6 11.7 %multiply_convert_fusion.3 = bf16[4,1024,1024]{1,2,0:T(8,128)(2,1)S(1)} fusion(f32[4,1024,1024]{1,2,0:T(8,128)} %get-tuple-element.317, f32[4,1024,1024]{1,2,0:T(8,128)} %copy-done.2, f32[4,1024]{1,0:T(4,128)S(1)} %copy-done.15), kind=kLoop, calls=%fused_computation.18.clone.1 | loop fusion | flops 12582912 | bytes 41959424 | tf_op jit(solution)/shard_map/while/body/eval_jaxpr/convert_element_type | solution.py:81
  434.8 11.9 %multiply_reduce_fusion.6 = (f32[4,1024]{1,0:T(4,128)}, f32[4,1024,1024]{1,2,0:T(8,128)}) fusion(f32[4,1024,1024]{1,2,0:T(8,128)S(1)} %fusion.123, f32[4,1024]{1,0:T(4,128)} %dynamic-slice_bitcast_fusion.2, bf16[4,1024,64]{1,2,0:T(8,128)(2,1)} %bitcast.147, bf16[4,1024,64]{1,2,0:T(8,128)(2,1)S(1)} %bitcast.145, ...), kind=kOutput, calls=%fused_computation.19.clone.1 | convolution fusion | flops 557838336 | bytes 35684352 | tf_op jit(solution)/shard_map/while/body/eval_jaxpr/hqd,hkd->hqk/dot_general | solution.py:36
  455.2 11.7 %multiply_convert_fusion.3 = bf16[4,1024,1024]{1,2,0:T(8,128)(2,1)S(1)} fusion(f32[4,1024,1024]{1,2,0:T(8,128)} %get-tuple-element.317, f32[4,1024,1024]{1,2,0:T(8,128)} %copy-done.2, f32[4,1024]{1,0:T(4,128)S(1)} %copy-done.15), kind=kLoop, calls=%fused_computation.18.clone.1 | loop fusion | flops 12582912 | bytes 41959424 | tf_op jit(solution)/shard_map/while/body/eval_jaxpr/convert_element_type | solution.py:81
  485.4 11.9 %multiply_reduce_fusion.6 = (f32[4,1024]{1,0:T(4,128)}, f32[4,1024,1024]{1,2,0:T(8,128)}) fusion(f32[4,1024,1024]{1,2,0:T(8,128)S(1)} %fusion.123, f32[4,1024]{1,0:T(4,128)} %dynamic-slice_bitcast_fusion.2, bf16[4,1024,64]{1,2,0:T(8,128)(2,1)} %bitcast.147, bf16[4,1024,64]{1,2,0:T(8,128)(2,1)S(1)} %bitcast.145, ...), kind=kOutput, calls=%fused_computation.19.clone.1 | convolution fusion | flops 557838336 | bytes 35684352 | tf_op jit(solution)/shard_map/while/body/eval_jaxpr/hqd,hkd->hqk/dot_general | solution.py:36
  505.8 11.7 %multiply_convert_fusion.3 = bf16[4,1024,1024]{1,2,0:T(8,128)(2,1)S(1)} fusion(f32[4,1024,1024]{1,2,0:T(8,128)} %get-tuple-element.317, f32[4,1024,1024]{1,2,0:T(8,128)} %copy-done.2, f32[4,1024]{1,0:T(4,128)S(1)} %copy-done.15), kind=kLoop, calls=%fused_computation.18.clone.1 | loop fusion | flops 12582912 | bytes 41959424 | tf_op jit(solution)/shard_map/while/body/eval_jaxpr/convert_element_type | solution.py:81
  546.2 43.9 %all-reduce = (f32[512]{0:T(512)}, f32[512]{0:T(512)}, f32[512]{0:T(512)}, f32[512]{0:T(512)}) all-reduce(f32[512]{0:T(512)S(1)} %copy-done.29, f32[512]{0:T(512)S(1)} %copy-done.30, f32[512]{0:T(512)S(1)} %copy-done.26, f32[512]{0:T(512)S(1)} %copy-done.27), channel_id=1, replica_groups=mesh['dp'=16,'mp'=2] {'dp','mp'}, use_global_device_ids=true, to_apply=%region_24.25 | all-reduce | flops 2048 | bytes 16384 | tf_op jit(solution)/shard_map/psum | solution.py:207
  590.2 163.3 %all-reduce.4.cloned.1.call-done = (f32[512,256]{0,1:T(8,128)}, f32[512,256]{0,1:T(8,128)}, f32[512,256]{0,1:T(8,128)}, f32[256,512]{1,0:T(8,128)}, f32[512,1024]{1,0:T(8,128)}, /*index=5*/f32[1024,512]{1,0:T(8,128)}) async-done(((f32[512,256]{0,1:T(8,128)}, f32[512,256]{0,1:T(8,128)}, f32[512,256]{0,1:T(8,128)}, f32[256,512]{1,0:T(8,128)}, f32[512,1024]{1,0:T(8,128)}, /*index=5*/f32[1024,512]{1,0:T(8,128)}), ...) | async-done | bytes 6291472 | tf_op jit(solution)/shard_map/psum | solution.py:204
  (277 shorter events, 298.4 us)
Async XLA Ops:
  7.2 160.7 %copy-start = (bf16[512,1024]{1,0:T(8,128)(2,1)S(1)}, bf16[512,1024]{1,0:T(8,128)(2,1)}, u32[]{:S(2)}) copy-start(bf16[512,1024]{1,0:T(8,128)(2,1)} %param.27) | copy-start | bytes 3145732
  7.2 18.8 %all-gather.5.cloned.1.call-start = ((), (), s32[]{:S(2)}) async-start(), calls=%async_computation.4 | async-start | bytes 6291456 | tf_op jit(solution)/shard_map/all_gather | solution.py:124
  7.9 138.4 %reduce-scatter.5.cloned.1.call-start = ((), (), s32[]{:S(2)}) async-start(), calls=%async_computation.5 | async-start | bytes 12582912 | tf_op jit(solution)/shard_map/reduce_scatter | solution.py:138
  11.6 22.1 %copy-start.20 = (bf16[512,768]{1,0:T(8,128)(2,1)}, bf16[512,768]{1,0:T(8,128)(2,1)S(1)}, u32[]{:S(2)}) copy-start(bf16[512,768]{1,0:T(8,128)(2,1)S(1)} %constant_dynamic-update-slice_fusion.2) | copy-start | bytes 2359300
  54.9 67.1 %copy-start.17 = (bf16[256,512]{1,0:T(8,128)(2,1)S(1)}, bf16[256,512]{1,0:T(8,128)(2,1)}, u32[]{:S(2)}) copy-start(bf16[256,512]{1,0:T(8,128)(2,1)} %param.24) | copy-start | bytes 786436
  128.1 18.2 %copy-start.9 = (bf16[2048,512]{1,0:T(8,128)(2,1)S(1)}, bf16[2048,512]{1,0:T(8,128)(2,1)}, u32[]{:S(2)}) copy-start(bf16[2048,512]{1,0:T(8,128)(2,1)} %param.19) | copy-start | bytes 6291460
  128.1 39.7 %all-gather.7.cloned.1.call-start = ((), (), s32[]{:S(2)}) async-start(), calls=%async_computation.6 | async-start | bytes 6291456 | tf_op jit(solution)/shard_map/all_gather | solution.py:150
  152.8 31.9 %copy-start.34 = (bf16[1024,512]{1,0:T(8,128)(2,1)S(1)}, bf16[1024,512]{1,0:T(8,128)(2,1)}, u32[]{:S(2)}) copy-start(bf16[1024,512]{1,0:T(8,128)(2,1)} %param.28) | copy-start | bytes 3145732
  152.8 56.7 %reduce-scatter.7.cloned.1.call-start = ((), (), s32[]{:S(2)}) async-start(), calls=%async_computation.7 | async-start | bytes 12582912 | tf_op jit(solution)/shard_map/reduce_scatter | solution.py:154
  191.3 18.2 %copy-start.12 = (bf16[2048,512]{1,0:T(8,128)(2,1)S(1)}, bf16[2048,512]{1,0:T(8,128)(2,1)}, u32[]{:S(2)}) copy-start(bf16[2048,512]{1,0:T(8,128)(2,1)} %param.20) | copy-start | bytes 6291460
  191.3 50.7 %all-gather.9.cloned.1.call-start = ((), (), s32[]{:S(2)}) async-start(), calls=%async_computation.8 | async-start | bytes 6291456 | tf_op jit(solution)/shard_map/all_gather | solution.py:165
  227.0 60.3 %reduce-scatter.9.cloned.1.call-start = ((), (), s32[]{:S(2)}) async-start(), calls=%async_computation.9 | async-start | bytes 12582912 | tf_op jit(solution)/shard_map/reduce_scatter | solution.py:171
  269.2 49.8 %all-gather.11.cloned.1.call-start = ((), (), s32[]{:S(2)}) async-start(), calls=%async_computation.10 | async-start | bytes 6291456 | tf_op jit(solution)/shard_map/all_gather | solution.py:179
  299.2 454.2 %all-reduce.4.cloned.1.call-start = ((), (), s32[]{:S(2)}) async-start(), calls=%async_computation.12 | async-start | bytes 12582912 | tf_op jit(solution)/shard_map/psum | solution.py:204
  299.3 10.6 %copy-start.33 = (bf16[4096,512]{1,0:T(8,128)(2,1)S(1)}, bf16[4096,512]{1,0:T(8,128)(2,1)}, u32[]{:S(2)}) copy-start(bf16[4096,512]{1,0:T(8,128)(2,1)} %all-gather.9.cloned.1.call-done) | copy-start | bytes 12582916
  333.7 11.9 %copy-start.2 = (f32[4,1024,1024]{1,2,0:T(8,128)}, f32[4,1024,1024]{1,2,0:T(8,128)S(1)}, u32[]{:S(2)}) copy-start(f32[4,1024,1024]{1,2,0:T(8,128)S(1)} %fusion.123) | copy-start | bytes 50331652 | tf_op jit(solution)/shard_map/while
  345.7 8.4 %copy-start.15 = (f32[4,1024]{1,0:T(4,128)S(1)}, f32[4,1024]{1,0:T(4,128)}, u32[]{:S(2)}) copy-start(f32[4,1024]{1,0:T(4,128)} %get-tuple-element.318) | copy-start | bytes 49156 | tf_op jit(solution)/shard_map/while
  384.2 11.9 %copy-start.2 = (f32[4,1024,1024]{1,2,0:T(8,128)}, f32[4,1024,1024]{1,2,0:T(8,128)S(1)}, u32[]{:S(2)}) copy-start(f32[4,1024,1024]{1,2,0:T(8,128)S(1)} %fusion.123) | copy-start | bytes 50331652 | tf_op jit(solution)/shard_map/while
  396.2 8.4 %copy-start.15 = (f32[4,1024]{1,0:T(4,128)S(1)}, f32[4,1024]{1,0:T(4,128)}, u32[]{:S(2)}) copy-start(f32[4,1024]{1,0:T(4,128)} %get-tuple-element.318) | copy-start | bytes 49156 | tf_op jit(solution)/shard_map/while
  434.8 11.9 %copy-start.2 = (f32[4,1024,1024]{1,2,0:T(8,128)}, f32[4,1024,1024]{1,2,0:T(8,128)S(1)}, u32[]{:S(2)}) copy-start(f32[4,1024,1024]{1,2,0:T(8,128)S(1)} %fusion.123) | copy-start | bytes 50331652 | tf_op jit(solution)/shard_map/while
  485.4 11.9 %copy-start.2 = (f32[4,1024,1024]{1,2,0:T(8,128)}, f32[4,1024,1024]{1,2,0:T(8,128)S(1)}, u32[]{:S(2)}) copy-start(f32[4,1024,1024]{1,2,0:T(8,128)S(1)} %fusion.123) | copy-start | bytes 50331652 | tf_op jit(solution)/shard_map/while
  536.6 230.7 %reduce-scatter.11.cloned.1.call-start = ((), (), s32[]{:S(2)}) async-start(), calls=%async_computation.11 | async-start | bytes 6291456 | tf_op jit(solution)/shard_map/reduce_scatter | solution.py:196
  545.5 221.8 %copy-start.23 = (f32[2048]{0:T(1024)S(1)}, f32[2048]{0:T(1024)}, u32[]{:S(2)}) copy-start(f32[2048]{0:T(1024)} %copy-done.22) | copy-start | bytes 24580
  759.6 13.9 %copy-start.14 = (f32[512,1024]{1,0:T(8,128)S(1)}, f32[512,1024]{1,0:T(8,128)}, u32[]{:S(2)}) copy-start(f32[512,1024]{1,0:T(8,128)} %get-tuple-element.379) | copy-start | bytes 6291460
  (37 other events, 140.5 us)
Sparse Core Ops, SparseCore 0:
  9.6 16.3 all-gather.4
  128.3 17.9 reduce-scatter.4
  152.9 14.8 all-gather.6
  191.5 17.9 reduce-scatter.6
  227.1 14.9 all-gather.8
  269.3 17.9 reduce-scatter.8
  299.3 14.8 all-gather.10
  536.7 216.6 all-reduce.3
  756.3 10.9 reduce-scatter.10
where the time goes:
time: 794 us; the launch traced here: 783 us
  waiting for transfers between devices  270 us (34%)
  matrix products  240 us (30%)
  other arithmetic  109 us (14%)
  local copies, waits for them, and re-layouts  104 us (13%)
  blocking collectives  43.9 us (6%)
  between operations  14.6 us (2%)
    psum x1, waiting for transfers between devices, on_device(): lax.psum((query_part, key_part, value_part, output_part, up_part, down_pa...  163 us
    dot_general x8, matrix products, masked_scores(): jnp.einsum('hqd,hkd->hqk', split_heads(query, head_size), split_heads(key...  60.9 us
    convert_element_type x4, other arithmetic, attend_backward(): grad_scores = (probs * (grad_probs - jnp.sum(probs * grad_probs, axis=-1,...  46.8 us
    psum x1, blocking collectives, on_device(): lax.psum((first_gain_part, first_bias_part, second_gain_part, second_bias...  43.9 us
    dot_general x4, matrix products, attend_backward(): jnp.einsum('hqk,hqd->hkd', probs.astype(jnp.bfloat16), grad_mixed, prefer...  33.7 us
    unnamed x75, local copies, waits for them, and re-layouts  31.6 us
    dynamic_slice x32, local copies, waits for them, and re-layouts, on_device(): lax.map(partial(attend_forward, head_size=HD), (query, keys, values, labe...  27.2 us
    dot_general x4, matrix products, attend_forward(): jnp.einsum('hqk,hkd->hqd', probs, split_heads(values, head_size), preferr...  19.9 us
  transfers between devices with their start and end apart: 9, of which 8 were waited for; matrix products, arithmetic and copies ran while one was open for 5% of the time, Pallas kernels for 0%

commit v1 on v0

v1 whole, which is shorter than its diff:
```python
from functools import partial

import jax
import jax.numpy as jnp
from jax import lax
from jax.sharding import PartitionSpec as P

HD = 64
LEN = 1024


norm_eps = 1e-05
masked_score = -1e30


def layer_norm(z, gain, bias):
    mean = jnp.mean(z, axis=-1, keepdims=True)
    centred = z - mean
    spread = jnp.mean(centred * centred, axis=-1, keepdims=True)
    return centred * lax.rsqrt(spread + norm_eps) * gain + bias


def smooth_gate(value):
    return jax.nn.gelu(value, approximate=True)


def split_heads(block, head_size):
    return block.reshape(block.shape[0], block.shape[1] // head_size, head_size).transpose(1, 0, 2)


def join_heads(block):
    return block.transpose(1, 0, 2).reshape(block.shape[1], block.shape[0] * block.shape[2])


def masked_scores(query, keys, labels, head_size):
    raw = jnp.einsum(
        "hqd,hkd->hqk",
        split_heads(query, head_size),
        split_heads(keys, head_size),
        preferred_element_type=jnp.float32,
    ) * head_size ** (-0.5)
    same = labels[:, None] == labels[None, :]
    return jnp.where(same[None], raw, masked_score)


def attend_forward(inputs, head_size):
    query, keys, values, labels = inputs
    scores = masked_scores(query, keys, labels, head_size)
    top = jnp.max(scores, axis=-1, keepdims=True)
    shifted = jnp.exp(scores - top)
    total = jnp.sum(shifted, axis=-1, keepdims=True)
    probs = (shifted / total).astype(jnp.bfloat16)
    mixed = jnp.einsum(
        "hqk,hkd->hqd", probs, split_heads(values, head_size), preferred_element_type=jnp.float32
    )
    live = (labels != 0).astype(jnp.float32)
    return (
        (join_heads(mixed) * live[:, None]).astype(jnp.bfloat16),
        (top + jnp.log(total))[..., 0],
    )


def attend_backward(inputs, head_size):
    query, keys, values, labels, upstream, log_totals = inputs
    scale = head_size ** (-0.5)
    scores = masked_scores(query, keys, labels, head_size)
    probs = jnp.exp(scores - log_totals[..., None])
    live = (labels != 0).astype(jnp.bfloat16)
    grad_mixed = split_heads(upstream * live[:, None], head_size)
    grad_values = jnp.einsum(
        "hqk,hqd->hkd", probs.astype(jnp.bfloat16), grad_mixed, preferred_element_type=jnp.float32
    )
    grad_probs = jnp.einsum(
        "hqd,hkd->hqk",
        grad_mixed,
        split_heads(values, head_size),
        preferred_element_type=jnp.float32,
    )
    grad_scores = (
        probs * (grad_probs - jnp.sum(probs * grad_probs, axis=-1, keepdims=True))
    ).astype(jnp.bfloat16)
    grad_query = (
        jnp.einsum(
            "hqk,hkd->hqd",
            grad_scores,
            split_heads(keys, head_size),
            preferred_element_type=jnp.float32,
        )
        * scale
    )
    grad_keys = (
        jnp.einsum(
            "hqk,hqd->hkd",
            grad_scores,
            split_heads(query, head_size),
            preferred_element_type=jnp.float32,
        )
        * scale
    )
    joined = jnp.concatenate(
        [join_heads(grad_query), join_heads(grad_keys), join_heads(grad_values)], axis=1
    )
    return joined.astype(jnp.bfloat16)


def swap_cores(block):
    return lax.ppermute(block, "mp", [(0, 1), (1, 0)])


def partner(block, mask, count):
    return lax.ppermute(block, "dp", [(i, i ^ mask) for i in range(count)])


def add_rounded(left, right):
    return (left.astype(jnp.float32) + right.astype(jnp.float32)).astype(jnp.bfloat16)


def sum_over_chips(blocks, orders, count):
    me = lax.axis_index("dp")
    order_of = jnp.arange(count) ^ me
    pieces = [
        block.reshape(count, block.shape[0] // count, block.shape[1])[order_of] for block in blocks
    ]
    positions = [list(range(count)) for _ in blocks]
    for step in range(len(orders[0])):
        for which, order in enumerate(orders):
            mask = order[step]
            stay = [i for i, p in enumerate(positions[which]) if not p & mask]
            by_position = {p: i for i, p in enumerate(positions[which])}
            move = [by_position[positions[which][i] ^ mask] for i in stay]
            block = pieces[which]
            sent = jnp.concatenate([block[i : i + 1] for i in move])
            kept = jnp.concatenate([block[i : i + 1] for i in stay])
            pieces[which] = add_rounded(kept, partner(sent, mask, count))
            positions[which] = [positions[which][i] for i in stay]
    for step in reversed(range(len(orders[0]))):
        for which, order in enumerate(orders):
            mask = order[step]
            got = partner(pieces[which], mask, count)
            pieces[which] = jnp.concatenate([pieces[which], got])
            positions[which] = positions[which] + [p ^ mask for p in positions[which]]
    out = []
    for which, block in enumerate(blocks):
        back = jnp.asarray([positions[which].index(p) for p in range(count)])
        out.append(pieces[which][back[order_of]].reshape(block.shape))
    return out


def on_device(
    normed_in,
    dual_in,
    query_weight,
    key_weight,
    value_weight,
    output_weight,
    first_gain,
    first_bias,
    up_weight,
    down_weight,
    second_gain,
    second_bias,
    segments,
    grad_normed_out,
    grad_dual_out,
    chips,
):
    rows = normed_in.shape[0]
    count = rows // LEN
    core = lax.axis_index("mp")
    half = query_weight.shape[1]
    own_joint = jnp.concatenate([query_weight, key_weight, value_weight], axis=1)
    other_joint = swap_cores(own_joint)
    joint_weight = jnp.concatenate(
        [
            part[:, i * half : (i + 1) * half]
            for i in range(3)
            for part in (own_joint, other_joint)
        ],
        axis=1,
    )
    full_output = jnp.concatenate([output_weight, swap_cores(output_weight)], axis=0)
    full_up = jnp.concatenate([up_weight, swap_cores(up_weight)], axis=1)
    full_down = jnp.concatenate([down_weight, swap_cores(down_weight)], axis=0)
    width = 2 * half
    qkv = jnp.dot(normed_in, joint_weight, preferred_element_type=jnp.float32).astype(jnp.bfloat16)
    blocks = qkv.reshape(count, LEN, 3 * width)
    query = blocks[:, :, :width]
    keys = blocks[:, :, width : 2 * width]
    values = blocks[:, :, 2 * width :]
    labels = lax.dynamic_slice(segments, (core * rows,), (rows,)).reshape(count, LEN)
    heads_out, log_totals = lax.map(
        partial(attend_forward, head_size=HD), (query, keys, values, labels)
    )
    heads_out = heads_out.reshape(rows, width)
    attn = jnp.dot(heads_out, full_output, preferred_element_type=jnp.float32)
    normed, first_pull = jax.vjp(
        layer_norm, normed_in.astype(jnp.float32) + attn, first_gain, first_bias
    )
    dual_mid = dual_in.astype(jnp.float32) + attn
    normed_low = normed.astype(jnp.bfloat16)
    pre = jnp.dot(normed_low, full_up, preferred_element_type=jnp.float32)
    hidden_full, gate_pull = jax.vjp(smooth_gate, pre)
    hidden = hidden_full.astype(jnp.bfloat16)
    ffn_out = jnp.dot(hidden, full_down, preferred_element_type=jnp.float32)
    normed_final, second_pull = jax.vjp(layer_norm, normed + ffn_out, second_gain, second_bias)
    dual_final = dual_mid + ffn_out
    upstream_dual = grad_dual_out.astype(jnp.float32)
    grad_mid, second_gain_part, second_bias_part = second_pull(grad_normed_out.astype(jnp.float32))
    grad_ffn = (grad_mid + upstream_dual).astype(jnp.bfloat16)
    grad_hidden = jnp.einsum("td,fd->tf", grad_ffn, full_down, preferred_element_type=jnp.float32)
    grad_pre = gate_pull(grad_hidden)[0].astype(jnp.bfloat16)
    down_part = jnp.einsum("tf,td->fd", hidden, grad_ffn, preferred_element_type=jnp.float32)
    up_part = jnp.einsum("td,tf->df", normed_low, grad_pre, preferred_element_type=jnp.float32)
    down_part = down_part.astype(jnp.bfloat16)
    up_part = up_part.astype(jnp.bfloat16)
    mid = down_part.shape[0] // 2
    down_half = add_rounded(down_part[:mid], swap_cores(down_part[mid:]))
    up_half = add_rounded(up_part[:, :mid], swap_cores(up_part[:, mid:]))
    bits = [1 << i for i in range(chips.bit_length() - 1)]
    orders = (tuple(bits), tuple([bits[1], bits[0]] + bits[2:]))
    down_total, up_total = sum_over_chips((down_half, up_half), orders, chips)
    grad_normed = grad_mid + jnp.einsum(
        "tf,df->td", grad_pre, full_up, preferred_element_type=jnp.float32
    )
    grad_first, first_gain_part, first_bias_part = first_pull(grad_normed)
    grad_attn = (grad_first + upstream_dual).astype(jnp.bfloat16)
    output_part = jnp.einsum("th,td->hd", heads_out, grad_attn, preferred_element_type=jnp.float32)
    grad_heads = jnp.einsum(
        "td,hd->th", grad_attn, full_output, preferred_element_type=jnp.float32
    ).astype(jnp.bfloat16)
    grad_joint = lax.map(
        partial(attend_backward, head_size=HD),
        (query, keys, values, labels, grad_heads.reshape(count, LEN, width), log_totals),
    )
    grad_joint = grad_joint.reshape(rows, 3 * width)
    joint_part = jnp.einsum(
        "td,tc->dc", normed_in, grad_joint, preferred_element_type=jnp.float32
    ).astype(jnp.bfloat16)
    own = jnp.concatenate(
        [joint_part[:, 2 * i * half : (2 * i + 1) * half] for i in range(3)], axis=1
    )
    other = jnp.concatenate(
        [joint_part[:, (2 * i + 1) * half : (2 * i + 2) * half] for i in range(3)], axis=1
    )
    joint_half = add_rounded(own, swap_cores(other))
    output_part = output_part.astype(jnp.bfloat16)
    output_half = add_rounded(output_part[:half], swap_cores(output_part[half:]))
    small = jnp.stack([first_gain_part, first_bias_part, second_gain_part, second_bias_part])
    small = jnp.concatenate([small, jnp.zeros((12, small.shape[1]), jnp.float32)])
    small = small + swap_cores(small)
    for mask in bits:
        small = small + partner(small, mask, chips)
    joint_total, output_total = sum_over_chips((joint_half, output_half), orders, chips)
    grad_stream = grad_first + jnp.einsum(
        "tc,dc->td", grad_joint, joint_weight, preferred_element_type=jnp.float32
    )
    joint_total = joint_total.astype(jnp.float32)
    return (
        normed_final.astype(jnp.bfloat16),
        dual_final.astype(jnp.bfloat16),
        grad_stream,
        joint_total[:, :half],
        joint_total[:, half : 2 * half],
        joint_total[:, 2 * half :],
        output_total.astype(jnp.float32),
        small[0],
        small[1],
        up_total.astype(jnp.float32),
        down_total.astype(jnp.float32),
        small[2],
        small[3],
    )


def solution(mesh):
    rows = P(("dp", "mp"), None)
    columns = P(None, "mp")
    return jax.shard_map(
        partial(on_device, chips=mesh.shape["dp"]),
        mesh=mesh,
        in_specs=(
            rows, rows, columns, columns, columns, P("mp", None), P(), P(),
            columns, P("mp", None), P(), P(), P("dp"), rows, rows,
        ),
        out_specs=(
            rows, rows, rows, columns, columns, columns, P("mp", None), P(), P(),
            columns, P("mp", None), P(), P(),
        ),
        check_vma=False,
    )
```

time: 794 us -> 673 us (0.85)
  waiting for transfers between devices: 270 us -> 43.4 us
  matrix products: 240 us -> 300 us
  starting transfers between devices: 1.16 us -> 49.8 us
  blocking collectives: 43.9 us -> 0 us
  local copies, waits for them, and re-layouts: 104 us -> 142 us
  other arithmetic: 109 us -> 126 us
  between operations: 14.6 us -> 2.06 us
    psum x1 -> x0, waiting for transfers between devices: 163 us -> none  [on_device(): lax.psum((query_part, key_part, value_part, output_part, up_part, down_pa...]
    reduce_scatter x4 -> x0, waiting for transfers between devices: 61.2 us -> none  [the longest x1 17.9 us: on_device(): lax.psum_scatter(jnp.einsum('tf,df->td', piece, up_weight, preferred_elem...]
    ppermute x0 -> x45, starting transfers between devices: none -> 49.8 us  [the longest x36 47.8 us: partner(): return lax.ppermute(block, 'dp', [(i, i ^ mask) for i in range(count)])]
    all_gather x4 -> x0, waiting for transfers between devices: 44.4 us -> none  [the longest x1 15 us: on_device(): grad_rows = lax.all_gather(grad_ffn, 'mp', axis=0, tiled=True)]
    psum x1 -> x0, blocking collectives: 43.9 us -> none  [on_device(): lax.psum((first_gain_part, first_bias_part, second_gain_part, second_bias...]
    ppermute x0 -> x45, waiting for transfers between devices: none -> 43.4 us  [the longest x36 43.3 us: partner(): return lax.ppermute(block, 'dp', [(i, i ^ mask) for i in range(count)])]
    dot_general x4 -> x2, matrix products: 9.51 us -> 47.8 us  [attend_backward(): jnp.einsum('hqd,hkd->hqk', grad_mixed, split_heads(values, head_size), pr...]
    unnamed x75 -> x148, local copies, waits for them, and re-layouts: 31.6 us -> 59.5 us
  transfers between devices with their start and end apart: 9 -> 45, of which waited for: 8 -> 21; matrix products, arithmetic and copies ran while one was open for 5% -> 74% of each run, Pallas kernels for 0% -> 0%
where the time goes in v1:
time: 673 us; the launch traced here: 665 us
  matrix products  300 us (45%)
  local copies, waits for them, and re-layouts  142 us (21%)
  other arithmetic  126 us (19%)
  starting transfers between devices  49.8 us (7%)
  waiting for transfers between devices  43.4 us (6%)
    unnamed x148, local copies, waits for them, and re-layouts  59.5 us
    convert_element_type x2, other arithmetic, attend_backward(): grad_scores = (probs * (grad_probs - jnp.sum(probs * grad_probs, axis=-1,...  56.4 us
    dot_general x4, matrix products, masked_scores(): jnp.einsum('hqd,hkd->hqk', split_heads(query, head_size), split_heads(key...  53.5 us
    dot_general x2, matrix products, attend_backward(): jnp.einsum('hqd,hkd->hqk', grad_mixed, split_heads(values, head_size), pr...  47.8 us
    ppermute x36, starting transfers between devices, partner(): return lax.ppermute(block, 'dp', [(i, i ^ mask) for i in range(count)])  47.8 us
    ppermute x36, waiting for transfers between devices, partner(): return lax.ppermute(block, 'dp', [(i, i ^ mask) for i in range(count)])  43.3 us
    dot_general x2, matrix products, attend_backward(): jnp.einsum('hqk,hqd->hkd', probs.astype(jnp.bfloat16), grad_mixed, prefer...  31.8 us
    reduce_sum x2, other arithmetic, attend_forward(): total = jnp.sum(shifted, axis=-1, keepdims=True)  28.4 us
  transfers between devices with their start and end apart: 45, of which 21 were waited for; matrix products, arithmetic and copies ran while one was open for 74% of the time, Pallas kernels for 0%

profile of v1, /device:TPU:0, one launch (start us, length us, event | category | flops | bytes accessed | tf_op | source)
XLA Modules:
  0.0 665.2 jit_solution(17873435828990204536)
XLA Ops:
  41.2 11.2 %reshape.425 = bf16[2,1024,1536]{1,0,2:T(2,128)(2,1)} reshape(bf16[2048,1536]{0,1:T(8,128)(2,1)} %fusion.29) | data formatting | bytes 12582912 | tf_op jit(solution)/shard_map/reshape | solution.py:186
  64.2 94.8 %while.22 = (s32[]{:T(128)}, bf16[2,1024,512]{2,1,0:T(8,128)(2,1)}, f32[2,8,1024]{2,1,0:T(8,128)S(1)}, s32[2,1024]{1,0:T(2,128)S(1)}, bf16[2,1024,512]{1,2,0:T(8...) while((s32[]{:T(128)}, bf16[2,1024,512]{2,1,0:T(8,128)(2,1)}, ...), condition=%wide.region_3.4_spmd, body=%wide.region_0.3_spmd.sunk | while | flops 2250237952 | bytes 124019304 | solution.py:191
  68.1 13.6 %fusion.120 = (f32[8,1024]{1,0:T(8,128)S(1)}, f32[8,1024,1024]{1,2,0:T(8,128)}) fusion(pred[1024,1024]{0,1:T(8,128)(4,1)S(1)} %broadcast_compare_fusion.4, bf16[8,1024,64]{1,2,0:T(8,128)(2,1)S(1)} %bitcast.182, bf16[8,1024,64]{1,2,0:T(8,128)(2,1)S(1)} %bitcast.181), kind=kOutput, calls=%fused_computation.13.clone.1 | convolution fusion | flops 1098899456 | bytes 36732928 | tf_op jit(solution)/shard_map/while/body/eval_jaxpr/hqd,hkd->hqk/dot_general | solution.py:36
  81.7 14.2 %fusion.121 = f32[8,1024]{1,0:T(8,128)S(1)} fusion(f32[8,1024,1024]{1,2,0:T(8,128)} %get-tuple-element.409, f32[8,1024]{1,0:T(8,128)S(1)} %get-tuple-element.410, pred[1024,1024]{0,1:T(8,128)(4,1)S(1)} %broadcast_compare_fusion.4), kind=kLoop, calls=%fused_computation.14.clone.1 | loop fusion | flops 33546240 | bytes 34668544 | tf_op jit(solution)/shard_map/while/body/eval_jaxpr/reduce_sum | solution.py:51
  95.9 13.9 %fusion.122 = f32[8,1024,64]{1,2,0:T(8,128)S(1)} fusion(bf16[8,1024,64]{1,2,0:T(8,128)(2,1)S(1)} %bitcast.188, f32[8,1024,1024]{1,2,0:T(8,128)} %get-tuple-element.409, f32[8,1024]{1,0:T(8,128)S(1)} %fusion.121, f32[8,1024]{1,0:T(8,128)S(1)} %get-tuple-element.410, pred[1024,1024]{0,1:T(8,128)(4,1)S(1)} %broadcast_compare_fusion.4), kind=kOutput, calls=%fused_computation.15.clone.1 | convolution fusion | flops 1115684864 | bytes 37814272 | tf_op jit(solution)/shard_map/while/body/eval_jaxpr/hqk,hkd->hqd/dot_general | solution.py:53
  115.4 13.6 %fusion.120 = (f32[8,1024]{1,0:T(8,128)S(1)}, f32[8,1024,1024]{1,2,0:T(8,128)}) fusion(pred[1024,1024]{0,1:T(8,128)(4,1)S(1)} %broadcast_compare_fusion.4, bf16[8,1024,64]{1,2,0:T(8,128)(2,1)S(1)} %bitcast.182, bf16[8,1024,64]{1,2,0:T(8,128)(2,1)S(1)} %bitcast.181), kind=kOutput, calls=%fused_computation.13.clone.1 | convolution fusion | flops 1098899456 | bytes 36732928 | tf_op jit(solution)/shard_map/while/body/eval_jaxpr/hqd,hkd->hqk/dot_general | solution.py:36
  129.0 14.2 %fusion.121 = f32[8,1024]{1,0:T(8,128)S(1)} fusion(f32[8,1024,1024]{1,2,0:T(8,128)} %get-tuple-element.409, f32[8,1024]{1,0:T(8,128)S(1)} %get-tuple-element.410, pred[1024,1024]{0,1:T(8,128)(4,1)S(1)} %broadcast_compare_fusion.4), kind=kLoop, calls=%fused_computation.14.clone.1 | loop fusion | flops 33546240 | bytes 34668544 | tf_op jit(solution)/shard_map/while/body/eval_jaxpr/reduce_sum | solution.py:51
  143.2 13.9 %fusion.122 = f32[8,1024,64]{1,2,0:T(8,128)S(1)} fusion(bf16[8,1024,64]{1,2,0:T(8,128)(2,1)S(1)} %bitcast.188, f32[8,1024,1024]{1,2,0:T(8,128)} %get-tuple-element.409, f32[8,1024]{1,0:T(8,128)S(1)} %fusion.121, f32[8,1024]{1,0:T(8,128)S(1)} %get-tuple-element.410, pred[1024,1024]{0,1:T(8,128)(4,1)S(1)} %broadcast_compare_fusion.4), kind=kOutput, calls=%fused_computation.15.clone.1 | convolution fusion | flops 1115684864 | bytes 37814272 | tf_op jit(solution)/shard_map/while/body/eval_jaxpr/hqk,hkd->hqd/dot_general | solution.py:53
  169.3 13.8 %multiply_convert_fusion.3 = (bf16[2048,2048]{1,0:T(8,128)(2,1)}, f32[2048,2048]{1,0:T(8,128)}) fusion(bf16[512,2048]{1,0:T(8,128)(2,1)S(1)} %constant_dynamic-update-slice_fusion.7, f32[2048,512]{0,1:T(8,128)S(1)} %get-tuple-element.189, f32[512]{0:T(512)S(1)} %copy-done.52, f32[512]{0:T(512)S(1)} %copy-done.50, f32[2048]{0:T(1024)S(1)} %fusion.39, ...), kind=kOutput, calls=%fused_computation.65 | convolution fusion | flops 4337958912 | bytes 31477760 | tf_op jit(solution)/shard_map/dot_general | solution.py:201
  185.8 14.4 %fusion.49 = (f32[2048]{0:T(1024)S(1)}, f32[2048,512]{0,1:T(8,128)S(1)}, bf16[2048,512]{0,1:T(8,128)(2,1)}) fusion(f32[512]{0:T(512)S(1)} %copy-done.52, f32[512]{0:T(512)S(1)} %copy-done.50, f32[2048]{0:T(1024)S(1)} %fusion.39, f32[2048,512]{0,1:T(8,128)} %copy-done.5, f32[2048]{0:T(1024)S(1)} %broadcast_multiply_fusion.1, ...), kind=kOutput, calls=%fused_computation.233 | convolution fusion | flops 4305451008 | bytes 27291648 | tf_op jit(solution)/shard_map/dot_general | solution.py:204
  207.8 22.3 %fusion.28 = bf16[2048,2048]{1,0:T(8,128)(2,1)} fusion(f32[2048,2048]{1,0:T(8,128)} %get-tuple-element.313, bf16[2048,512]{0,1:T(8,128)(2,1)} %get-tuple-element.201, bf16[2048,512]{1,0:T(8,128)(2,1)} %copy-done.36), kind=kOutput, calls=%fused_computation.64 | convolution fusion | flops 4378853376 | bytes 29360128 | tf_op jit(solution)/shard_map/td,fd->tf/dot_general | solution.py:210
  230.1 9.7 %multiply_reduce_fusion.1 = (f32[512]{0:T(512)S(1)}, f32[2048]{0:T(1024)S(1)}, f32[512]{0:T(512)S(1)}, f32[2048,512]{0,1:T(8,128)S(1)}) fusion(f32[2048,512]{0,1:T(8,128)S(1)} %copy-done.6, f32[2048]{0:T(1024)S(1)} %fusion.39, f32[2048]{0:T(1024)S(1)} %broadcast_multiply_fusion.1, f32[512]{0:T(512)S(1)} %copy-done.50, bf16[2048,2048]{1,0:T(8,128)(2,1)} %fusion.28, ...), kind=kOutput, calls=%fused_computation.81 | convolution fusion | flops 4312790016 | bytes 25231360 | tf_op jit(solution)/shard_map/tf,df->td/dot_general | solution.py:222
  252.9 233.3 %while.23 = (s32[]{:T(128)}, bf16[2,1024,1536]{2,1,0:T(8,128)(2,1)}, s32[2,1024]{1,0:T(2,128)S(1)}, bf16[2,1024,512]{1,2,0:T(8,128)(2,1)}, bf16[2,1024,512]{1,2,...) while((s32[]{:T(128)}, ...), condition=%wide.region_14.15_spmd, body=%wide.region_12.14_spmd.sunk | while | flops 5508687872 | bytes 379837152 | solution.py:231
  257.3 13.2 %fusion.133 = f32[8,1024,1024]{1,2,0:T(8,128)} fusion(bf16[8,1024,64]{1,2,0:T(8,128)(2,1)S(1)} %bitcast.179, bf16[8,1024,64]{1,2,0:T(8,128)(2,1)S(1)} %bitcast.177), kind=kOutput, calls=%fused_computation.249.clone.1 | convolution fusion | flops 1073741824 | bytes 35651584 | tf_op jit(solution)/shard_map/while/body/eval_jaxpr/hqd,hkd->hqk/dot_general | solution.py:36
  274.4 23.9 %multiply_reduce_fusion.6 = (f32[8,1024]{1,0:T(8,128)S(1)}, f32[8,1024,1024]{1,2,0:T(8,128)}) fusion(f32[8,1024,1024]{1,2,0:T(8,128)} %fusion.133, f32[8,1024]{1,0:T(8,128)S(1)} %dynamic-slice_bitcast_fusion.2, pred[1024,1024]{0,1:T(8,128)(4,1)S(1)} %broadcast_compare_fusion.5, bf16[8,1024,64]{1,2,0:T(8,128)(2,1)} %bitcast.183, ...), kind=kOutput, calls=%fused_computation.29.clone.1 | convolution fusion | flops 1116200960 | bytes 70322176 | tf_op jit(solution)/shard_map/while/body/eval_jaxpr/hqd,hkd->hqk/dot_general | solution.py:73
  298.3 28.2 %multiply_convert_fusion.7 = bf16[8,1024,1024]{1,2,0:T(8,128)(2,1)} fusion(f32[8,1024,1024]{1,2,0:T(8,128)} %get-tuple-element.421, f32[8,1024,1024]{1,2,0:T(8,128)} %fusion.133, f32[8,1024]{1,0:T(8,128)S(1)} %get-tuple-element.422, f32[8,1024]{1,0:T(8,128)S(1)} %dynamic-slice_bitcast_fusion.2, pred[1024,1024]{0,1:T(8,128)(4,1)S(1)} %broadcast_compare_fusion.5), kind=kLoop, calls=%fused_computation.28.clone.1 | loop fusion | flops 50331648 | bytes 85000192 | tf_op jit(solution)/shard_map/while/body/eval_jaxpr/convert_element_type | solution.py:81
  326.6 9.9 %multiply_convert_fusion.9 = bf16[8,1024,64]{1,2,0:T(8,128)(2,1)} fusion(bf16[8,1024,64]{1,2,0:T(8,128)(2,1)S(1)} %bitcast.178, bf16[8,1024,1024]{1,2,0:T(8,128)(2,1)} %multiply_convert_fusion.7), kind=kOutput, calls=%fused_computation.36.clone.1 | convolution fusion | flops 1074790400 | bytes 18874368 | tf_op jit(solution)/shard_map/while/body/eval_jaxpr/hqk,hkd->hqd/dot_general | solution.py:83
  345.0 15.9 %fusion.134 = bf16[8,1024,64]{1,2,0:T(8,128)(2,1)} fusion(f32[8,1024,1024]{1,2,0:T(8,128)} %fusion.133, f32[8,1024]{1,0:T(8,128)S(1)} %dynamic-slice_bitcast_fusion.2, pred[1024,1024]{0,1:T(8,128)(4,1)S(1)} %broadcast_compare_fusion.5, bf16[1024,8,64]{0,2,1:T(8,128)(2,1)S(1)} %bitcast.185, bf16[1024]{0:T(1024)(128)(2,1)S(1)} %compare_convert_fusion.5), kind=kOutput, calls=%fused_computation.38.clone.1 | convolution fusion | flops 1108344832 | bytes 36734976 | tf_op jit(solution)/shard_map/while/body/eval_jaxpr/hqk,hqd->hkd/dot_general | solution.py:70
  373.6 13.2 %fusion.133 = f32[8,1024,1024]{1,2,0:T(8,128)} fusion(bf16[8,1024,64]{1,2,0:T(8,128)(2,1)S(1)} %bitcast.179, bf16[8,1024,64]{1,2,0:T(8,128)(2,1)S(1)} %bitcast.177), kind=kOutput, calls=%fused_computation.249.clone.1 | convolution fusion | flops 1073741824 | bytes 35651584 | tf_op jit(solution)/shard_map/while/body/eval_jaxpr/hqd,hkd->hqk/dot_general | solution.py:36
  390.8 23.9 %multiply_reduce_fusion.6 = (f32[8,1024]{1,0:T(8,128)S(1)}, f32[8,1024,1024]{1,2,0:T(8,128)}) fusion(f32[8,1024,1024]{1,2,0:T(8,128)} %fusion.133, f32[8,1024]{1,0:T(8,128)S(1)} %dynamic-slice_bitcast_fusion.2, pred[1024,1024]{0,1:T(8,128)(4,1)S(1)} %broadcast_compare_fusion.5, bf16[8,1024,64]{1,2,0:T(8,128)(2,1)} %bitcast.183, ...), kind=kOutput, calls=%fused_computation.29.clone.1 | convolution fusion | flops 1116200960 | bytes 70322176 | tf_op jit(solution)/shard_map/while/body/eval_jaxpr/hqd,hkd->hqk/dot_general | solution.py:73
  414.7 28.2 %multiply_convert_fusion.7 = bf16[8,1024,1024]{1,2,0:T(8,128)(2,1)} fusion(f32[8,1024,1024]{1,2,0:T(8,128)} %get-tuple-element.421, f32[8,1024,1024]{1,2,0:T(8,128)} %fusion.133, f32[8,1024]{1,0:T(8,128)S(1)} %get-tuple-element.422, f32[8,1024]{1,0:T(8,128)S(1)} %dynamic-slice_bitcast_fusion.2, pred[1024,1024]{0,1:T(8,128)(4,1)S(1)} %broadcast_compare_fusion.5), kind=kLoop, calls=%fused_computation.28.clone.1 | loop fusion | flops 50331648 | bytes 85000192 | tf_op jit(solution)/shard_map/while/body/eval_jaxpr/convert_element_type | solution.py:81
  442.9 9.9 %multiply_convert_fusion.9 = bf16[8,1024,64]{1,2,0:T(8,128)(2,1)} fusion(bf16[8,1024,64]{1,2,0:T(8,128)(2,1)S(1)} %bitcast.178, bf16[8,1024,1024]{1,2,0:T(8,128)(2,1)} %multiply_convert_fusion.7), kind=kOutput, calls=%fused_computation.36.clone.1 | convolution fusion | flops 1074790400 | bytes 18874368 | tf_op jit(solution)/shard_map/while/body/eval_jaxpr/hqk,hkd->hqd/dot_general | solution.py:83
  461.3 15.9 %fusion.134 = bf16[8,1024,64]{1,2,0:T(8,128)(2,1)} fusion(f32[8,1024,1024]{1,2,0:T(8,128)} %fusion.133, f32[8,1024]{1,0:T(8,128)S(1)} %dynamic-slice_bitcast_fusion.2, pred[1024,1024]{0,1:T(8,128)(4,1)S(1)} %broadcast_compare_fusion.5, bf16[1024,8,64]{0,2,1:T(8,128)(2,1)S(1)} %bitcast.185, bf16[1024]{0:T(1024)(128)(2,1)S(1)} %compare_convert_fusion.5), kind=kOutput, calls=%fused_computation.38.clone.1 | convolution fusion | flops 1108344832 | bytes 36734976 | tf_op jit(solution)/shard_map/while/body/eval_jaxpr/hqk,hqd->hkd/dot_general | solution.py:70
  499.9 9.6 %convolution_convert_fusion.2 = bf16[512,2048]{1,0:T(8,128)(2,1)S(1)} fusion(bf16[2048,2048]{1,0:T(8,128)(2,1)} %fusion.28, f32[2048,512]{0,1:T(8,128)} %copy-done.5, f32[512]{0:T(512)S(1)} %copy-done.53, f32[512]{0:T(512)S(1)} %copy-done.51, f32[2048]{0:T(1024)S(1)} %copy-done.44, f32[2048]{0:T(1024)S(1)} %copy-done.39), kind=kOutput, calls=%fused_computation.94 | convolution fusion | flops 4301258752 | bytes 14700544 | tf_op jit(solution)/shard_map/td,tf->df/dot_general | solution.py:213
  (427 shorter events, 315.5 us)
Async XLA Ops:
  2.7 25.0 %collective-permute-start = (bf16[512,768]{1,0:T(8,128)(2,1)}, bf16[512,768]{1,0:T(8,128)(2,1)}, u32[]{:S(2)}, u32[]{:S(2)}) collective-permute-start(bf16[512,768]{1,0:T(8,128)(2,1)} %pad_maximum_fusion.1), channel_id=1, source_target_pairs={{0,1},{1,0},{2,3},{3,2},{4,5},{5,4},{6,7},{7,6},{8,9},{9,8},{10,11... | collective-permute-start | bytes 2359304 | tf_op jit(solution)/shard_map/ppermute | solution.py:107
  3.2 22.9 %collective-permute-start.1 = (bf16[256,512]{1,0:T(8,128)(2,1)}, bf16[256,512]{1,0:T(8,128)(2,1)}, u32[]{:S(2)}, u32[]{:S(2)}) collective-permute-start(bf16[256,512]{1,0:T(8,128)(2,1)} %param.28), channel_id=1, source_target_pairs={{0,1},{1,0},{2,3},{3,2},{4,5},{5,4},{6,7},{7,6},{8,9},{9,8},{10,11... | collective-permute-start | bytes 786440 | tf_op jit(solution)/shard_map/ppermute | solution.py:107
  3.2 162.2 %collective-permute-start.2 = (bf16[512,1024]{1,0:T(8,128)(2,1)}, bf16[512,1024]{1,0:T(8,128)(2,1)}, u32[]{:S(2)}, u32[]{:S(2)}) collective-permute-start(bf16[512,1024]{1,0:T(8,128)(2,1)} %param.31), channel_id=1, source_target_pairs={{0,1},{1,0},{2,3},{3,2},{4,5},{5,4},{6,7},{7,6},{8,9},{9,8},{10,11... | collective-permute-start | bytes 3145736 | tf_op jit(solution)/shard_map/ppermute | solution.py:107
  3.7 179.5 %collective-permute-start.3 = (bf16[1024,512]{1,0:T(8,128)(2,1)}, bf16[1024,512]{1,0:T(8,128)(2,1)}, u32[]{:S(2)}, u32[]{:S(2)}) collective-permute-start(bf16[1024,512]{1,0:T(8,128)(2,1)} %param.32), channel_id=1, source_target_pairs={{0,1},{1,0},{2,3},{3,2},{4,5},{5,4},{6,7},{7,6},{8,9},{9,8},{10,11... | collective-permute-start | bytes 3145736 | tf_op jit(solution)/shard_map/ppermute | solution.py:107
  251.7 257.8 %collective-permute-start.22 = (f32[16,512]{1,0:T(8,128)}, f32[16,512]{1,0:T(8,128)}, u32[]{:S(2)}, u32[]{:S(2)}) collective-permute-start(f32[16,512]{1,0:T(8,128)} %concatenate.204), channel_id=1, source_target_pairs={{0,1},{1,0},{2,3},{3,2},{4,5},{5,4},{6,7},{7,6},{8,9},{9,8},{10,11... | collective-permute-start | bytes 98312 | tf_op jit(solution)/shard_map/ppermute | solution.py:107
  252.8 242.0 %collective-permute-start.13 = (bf16[256,512]{1,0:T(8,128)(2,1)}, bf16[256,512]{1,0:T(8,128)(2,1)}, u32[]{:S(2)}, u32[]{:S(2)}) collective-permute-start(bf16[256,512]{1,0:T(8,128)(2,1)} %slice.614), channel_id=1, source_target_pairs={{0,1},{1,0},{2,3},{3,2},{4,5},{5,4},{6,7},{7,6},{8,9},{9,8},{10,11... | collective-permute-start | bytes 786440 | tf_op jit(solution)/shard_map/ppermute | solution.py:107
  496.8 15.4 %collective-permute-start.14 = (bf16[8,16,512]{2,1,0:T(8,128)(2,1)S(1)}, bf16[8,16,512]{2,1,0:T(8,128)(2,1)S(1)}, u32[]{:S(2)}, u32[]{:S(2)}) collective-permute-start(bf16[8,16,512]{2,1,0:T(8,128)(2,1)S(1)} %pad_maximum_fusion.13), channel_id=1, source_target_pairs={{0,4},{2,6},{4,0},{6,2},{8,12},{10,14},{12,8},{14,10},{16,20},{18,... | collective-permute-start | bytes 393224 | tf_op jit(solution)/shard_map/ppermute | solution.py:111
  517.6 8.3 %collective-permute-start.24 = (f32[16,512]{1,0:T(8,128)S(1)}, f32[16,512]{1,0:T(8,128)S(1)}, u32[]{:S(2)}, u32[]{:S(2)}) collective-permute-start(f32[16,512]{1,0:T(8,128)S(1)} %add.254), channel_id=1, source_target_pairs={{0,4},{2,6},{4,0},{6,2},{8,12},{10,14},{12,8},{14,10},{16,20},{18,... | collective-permute-start | bytes 98312 | tf_op jit(solution)/shard_map/ppermute | solution.py:111
  517.7 8.3 %collective-permute-start.16 = (bf16[2,16,512]{2,1,0:T(8,128)(2,1)S(1)}, bf16[2,16,512]{2,1,0:T(8,128)(2,1)S(1)}, u32[]{:S(2)}, u32[]{:S(2)}) collective-permute-start(bf16[2,16,512]{2,1,0:T(8,128)(2,1)S(1)} %pad_maximum_fusion.23), channel_id=1, source_target_pairs={{0,8},{2,10},{4,12},{6,14},{8,0},{10,2},{12,4},{14,6},{16,24},{18,... | collective-permute-start | bytes 98312 | tf_op jit(solution)/shard_map/ppermute | solution.py:111
  524.3 47.0 %collective-permute-start.36 = (bf16[1024,512]{1,0:T(8,128)(2,1)}, bf16[1024,512]{1,0:T(8,128)(2,1)}, u32[]{:S(2)}, u32[]{:S(2)}) collective-permute-start(bf16[1024,512]{1,0:T(8,128)(2,1)} %slice.664), channel_id=1, source_target_pairs={{0,1},{1,0},{2,3},{3,2},{4,5},{5,4},{6,7},{7,6},{8,9},{9,8},{10,11... | collective-permute-start | bytes 3145736 | tf_op jit(solution)/shard_map/ppermute | solution.py:107
  525.4 57.2 %collective-permute-start.27 = (bf16[512,1024]{1,0:T(8,128)(2,1)}, bf16[512,1024]{1,0:T(8,128)(2,1)S(1)}, u32[]{:S(2)}, u32[]{:S(2)}) collective-permute-start(bf16[512,1024]{1,0:T(8,128)(2,1)} %slice.640), channel_id=1, source_target_pairs={{0,1},{1,0},{2,3},{3,2},{4,5},{5,4},{6,7},{7,6},{8,9},{9,8},{10,11... | collective-permute-start | bytes 3145736 | tf_op jit(solution)/shard_map/ppermute | solution.py:107
  530.1 17.4 %collective-permute-start.26 = (f32[16,512]{1,0:T(8,128)S(1)}, f32[16,512]{1,0:T(8,128)S(1)}, u32[]{:S(2)}, u32[]{:S(2)}) collective-permute-start(f32[16,512]{1,0:T(8,128)S(1)} %add.256), channel_id=1, source_target_pairs={{0,16},{2,18},{4,20},{6,22},{8,24},{10,26},{12,28},{14,30},{16,0},... | collective-permute-start | bytes 98312 | tf_op jit(solution)/shard_map/ppermute | solution.py:111
  533.1 14.4 %collective-permute-start.18 = (bf16[1,16,512]{2,1,0:T(8,128)(2,1)S(1)}, bf16[1,16,512]{2,1,0:T(8,128)(2,1)S(1)}, u32[]{:S(2)}, u32[]{:S(2)}) collective-permute-start(bf16[1,16,512]{2,1,0:T(8,128)(2,1)S(1)} %get-tuple-element.181), channel_id=1, source_target_pairs={{0,16},{2,18},{4,20},{6,22},{8,24},{10,26},{12,28},{14,30},{16,0},... | collective-permute-start | bytes 49160 | tf_op jit(solution)/shard_map/ppermute | solution.py:111
  535.3 27.2 %collective-permute-start.4 = (bf16[512,768]{0,1:T(8,128)(2,1)}, bf16[512,768]{0,1:T(8,128)(2,1)}, u32[]{:S(2)}, u32[]{:S(2)}) collective-permute-start(bf16[512,768]{0,1:T(8,128)(2,1)} %pad_maximum_fusion.2), channel_id=1, source_target_pairs={{0,1},{1,0},{2,3},{3,2},{4,5},{5,4},{6,7},{7,6},{8,9},{9,8},{10,11... | collective-permute-start | bytes 2359304 | tf_op jit(solution)/shard_map/ppermute | solution.py:107
  569.8 9.7 %collective-permute-start.5 = (bf16[8,32,768]{2,1,0:T(8,128)(2,1)}, bf16[8,32,768]{2,1,0:T(8,128)(2,1)}, u32[]{:S(2)}, u32[]{:S(2)}) collective-permute-start(bf16[8,32,768]{2,1,0:T(8,128)(2,1)} %constant_dynamic-update-slice_fusion.19), channel_id=1, source_target_pairs={{0,2},{2,0},{4,6},{6,4},{8,10},{10,8},{12,14},{14,12},{16,18},{18,... | collective-permute-start | bytes 1179656 | tf_op jit(solution)/shard_map/ppermute | solution.py:111
  578.9 20.6 %collective-permute-start.37 = (bf16[8,64,512]{2,1,0:T(8,128)(2,1)}, bf16[8,64,512]{2,1,0:T(8,128)(2,1)}, u32[]{:S(2)}, u32[]{:S(2)}) collective-permute-start(bf16[8,64,512]{2,1,0:T(8,128)(2,1)} %constant_dynamic-update-slice_fusion.50), channel_id=1, source_target_pairs={{0,2},{2,0},{4,6},{6,4},{8,10},{10,8},{12,14},{14,12},{16,18},{18,... | collective-permute-start | bytes 1572872 | tf_op jit(solution)/shard_map/ppermute | solution.py:111
  594.0 11.1 %collective-permute-start.28 = (bf16[8,32,1024]{2,1,0:T(8,128)(2,1)S(1)}, bf16[8,32,1024]{2,1,0:T(8,128)(2,1)S(1)}, u32[]{:S(2)}, u32[]{:S(2)}) collective-permute-start(bf16[8,32,1024]{2,1,0:T(8,128)(2,1)S(1)} %pad_maximum_fusion.3), channel_id=1, source_target_pairs={{0,4},{2,6},{4,0},{6,2},{8,12},{10,14},{12,8},{14,10},{16,20},{18,... | collective-permute-start | bytes 1572872 | tf_op jit(solution)/shard_map/ppermute | solution.py:111
  597.9 10.8 %collective-permute-start.9 = (bf16[1,32,768]{2,1,0:T(8,128)(2,1)S(1)}, bf16[1,32,768]{2,1,0:T(8,128)(2,1)S(1)}, u32[]{:S(2)}, u32[]{:S(2)}) collective-permute-start(bf16[1,32,768]{2,1,0:T(8,128)(2,1)S(1)} %get-tuple-element.183), channel_id=1, source_target_pairs={{0,16},{2,18},{4,20},{6,22},{8,24},{10,26},{12,28},{14,30},{16,0},... | collective-permute-start | bytes 147464 | tf_op jit(solution)/shard_map/ppermute | solution.py:111
  600.9 14.8 %collective-permute-start.38 = (bf16[4,64,512]{2,1,0:T(8,128)(2,1)S(1)}, bf16[4,64,512]{2,1,0:T(8,128)(2,1)S(1)}, u32[]{:S(2)}, u32[]{:S(2)}) collective-permute-start(bf16[4,64,512]{2,1,0:T(8,128)(2,1)S(1)} %pad_maximum_fusion.9), channel_id=1, source_target_pairs={{0,4},{2,6},{4,0},{6,2},{8,12},{10,14},{12,8},{14,10},{16,20},{18,... | collective-permute-start | bytes 786440 | tf_op jit(solution)/shard_map/ppermute | solution.py:111
  605.4 10.8 %collective-permute-start.29 = (bf16[4,32,1024]{2,1,0:T(8,128)(2,1)S(1)}, bf16[4,32,1024]{2,1,0:T(8,128)(2,1)S(1)}, u32[]{:S(2)}, u32[]{:S(2)}) collective-permute-start(bf16[4,32,1024]{2,1,0:T(8,128)(2,1)S(1)} %pad_maximum_fusion.7), channel_id=1, source_target_pairs={{0,2},{2,0},{4,6},{6,4},{8,10},{10,8},{12,14},{14,12},{16,18},{18,... | collective-permute-start | bytes 786440 | tf_op jit(solution)/shard_map/ppermute | solution.py:111
  619.2 22.5 %collective-permute-start.12 = (bf16[8,32,768]{2,1,0:T(8,128)(2,1)S(1)}, bf16[8,32,768]{2,1,0:T(8,128)(2,1)S(1)}, u32[]{:S(2)}, u32[]{:S(2)}) collective-permute-start(bf16[8,32,768]{2,1,0:T(8,128)(2,1)S(1)} %pad_maximum_fusion.6), channel_id=1, source_target_pairs={{0,2},{2,0},{4,6},{6,4},{8,10},{10,8},{12,14},{14,12},{16,18},{18,... | collective-permute-start | bytes 1179656 | tf_op jit(solution)/shard_map/ppermute | solution.py:111
  641.4 8.8 %collective-permute-start.34 = (bf16[4,32,1024]{2,1,0:T(8,128)(2,1)}, bf16[4,32,1024]{2,1,0:T(8,128)(2,1)}, u32[]{:S(2)}, u32[]{:S(2)}) collective-permute-start(bf16[4,32,1024]{2,1,0:T(8,128)(2,1)} %pad_maximum_fusion.8), channel_id=1, source_target_pairs={{0,2},{2,0},{4,6},{6,4},{8,10},{10,8},{12,14},{14,12},{16,18},{18,... | collective-permute-start | bytes 786440 | tf_op jit(solution)/shard_map/ppermute | solution.py:111
  647.6 9.2 %collective-permute-start.44 = (bf16[8,64,512]{2,1,0:T(8,128)(2,1)S(1)}, bf16[8,64,512]{2,1,0:T(8,128)(2,1)S(1)}, u32[]{:S(2)}, u32[]{:S(2)}) collective-permute-start(bf16[8,64,512]{2,1,0:T(8,128)(2,1)S(1)} %pad_maximum_fusion.5), channel_id=1, source_target_pairs={{0,2},{2,0},{4,6},{6,4},{8,10},{10,8},{12,14},{14,12},{16,18},{18,... | collective-permute-start | bytes 1572872 | tf_op jit(solution)/shard_map/ppermute | solution.py:111
  652.0 9.5 %collective-permute-start.35 = (bf16[8,32,1024]{2,1,0:T(8,128)(2,1)}, bf16[8,32,1024]{2,1,0:T(8,128)(2,1)}, u32[]{:S(2)}, u32[]{:S(2)}) collective-permute-start(bf16[8,32,1024]{2,1,0:T(8,128)(2,1)} %pad_maximum_fusion.4), channel_id=1, source_target_pairs={{0,4},{2,6},{4,0},{6,2},{8,12},{10,14},{12,8},{14,10},{16,20},{18,... | collective-permute-start | bytes 1572872 | tf_op jit(solution)/shard_map/ppermute | solution.py:111
  (81 other events, 883.6 us)
